TPU v7x, 32 devices: a whole 2x2x4 slice. The times are simulated.
32 devices in a mesh: parts: 2 (over x), chan: 16 (over z, y, core).
Axes of the slice: x: 2, y: 2, z: 4, core: 2. Of those that a mesh axis runs over, the one named last changes fastest.
Arguments:
- spectra: bfloat16 [1024, 8, 1024], P(('parts', 'chan')), parts along dimension 0, may hold values from -8 to 8
- source_blocks: int32 [4, 2], P('parts'), parts along dimension 0, may hold values from 0 to 15
- window_valid: int32 [16], P('parts'), parts along dimension 0, may hold values 0 or 1
Outputs:
- correlations: bfloat16 [2, 2, 32, 1024, 512], P(None, None, None, ('parts', 'chan')), parts along dimension 3
There are 2 independent parts, one for each index of `parts`. A program takes and returns all parts, laid end to end along the dimension named above; each array names one. Nothing has to cross between parts.
All inputs are finite; a program needn't handle non-finite values. Where the computation divides by a largest or mean magnitude, that divisor is 1e-20 or more.
Results may differ from a plain program's by a relative error of at most 0.0045.
Values may be sent and summed in bfloat16 or wider, within the bound.
A program may use at most 192 MiB of HBM per device.

v0:
```python
import math

import jax
import jax.numpy as jnp
from jax import lax
from jax.sharding import PartitionSpec as P

SOURCE = 32
LAGS = 512


def from_root(block, axis, source):
    block = jnp.where(lax.axis_index(axis) == source, block, jnp.zeros_like(block))
    return lax.psum(block, axis)


def build_table(bins, lags):
    freq = jnp.arange(bins, dtype=jnp.int32)[:, None]
    shifted = jnp.arange(lags, dtype=jnp.int32)[None, :] - lags // 2
    phase = jnp.remainder(freq * shifted, 2 * bins).astype(jnp.float32)
    theta = phase * (2.0 * math.pi / (2 * bins))
    weight = jnp.where(freq == 0, 1.0, 2.0).astype(jnp.float32) / (2 * bins)
    return jnp.concatenate([weight * jnp.cos(theta), -weight * jnp.sin(theta)], axis=0).astype(
        jnp.bfloat16
    )


def shards(spectra, source_blocks, window_valid):
    receivers, windows, width = spectra.shape
    bins = width // 2
    per_device = receivers // SOURCE
    lag_table = build_table(bins, LAGS)
    window_mask = window_valid.astype(jnp.bfloat16)[None, :, None]
    real_rcv = spectra[..., :bins]
    imag_rcv = spectra[..., bins:]
    num_steps = source_blocks.shape[0]
    traces_all = []
    for step in range(num_steps):
        for slot in range(2):
            block_index = source_blocks[step, slot]
            source = from_root(spectra, "chan", block_index // per_device)
            masked = source * window_mask
            stacked_src = jnp.concatenate([masked[..., :bins], masked[..., bins:]], axis=0)
            with_real = jnp.einsum(
                "swf,rwf->srf", stacked_src, real_rcv, preferred_element_type=jnp.float32
            )
            with_imag = jnp.einsum(
                "swf,rwf->srf", stacked_src, imag_rcv, preferred_element_type=jnp.float32
            )
            real_part = with_real[:SOURCE] + with_imag[SOURCE:]
            imag_part = with_imag[:SOURCE] - with_real[SOURCE:]
            cross = jnp.concatenate([real_part, imag_part], axis=2).astype(jnp.bfloat16)
            flat = cross.reshape(SOURCE * receivers, width)
            traces = jnp.dot(flat, lag_table, preferred_element_type=jnp.float32).reshape(
                SOURCE, receivers, LAGS
            )
            traces, local_peak = (traces, jnp.max(jnp.abs(traces), axis=(1, 2)))
            global_peak = lax.pmax(local_peak, "chan")
            traces_all.append((traces / (global_peak[:, None, None] + 1e-06)).astype(jnp.bfloat16))
    stacked = jnp.stack(traces_all, axis=0)
    return stacked.reshape(num_steps, 2, SOURCE, receivers, LAGS)


def solution(mesh):
    placed = (P(("parts", "chan"), None, None), P("parts", None), P("parts"))
    return jax.shard_map(
        shards,
        mesh=mesh,
        in_specs=placed,
        out_specs=P(None, None, None, ("parts", "chan"), None),
        check_vma=False,
    )
```

profile of v0, /device:TPU:0, one launch (start us, length us, event | category | flops | bytes accessed | tf_op | source)
XLA Modules:
  0.0 359.4 jit_solution(7590580880067634399)
XLA Ops:
  6.5 1.4 fusion.67
  10.5 2.7 copy.28
  13.2 3.5 broadcast_select_fusion.3
  17.3 4.4 %multiply_convert_fusion.1 = (bf16[512,512]{1,0:T(8,128)(2,1)S(1)}, bf16[512,512]{1,0:T(8,128)(2,1)S(1)}) fusion(s32[512]{0:T(512)S(1)} %iota_add_fusion, f32[512]{0:T(512)S(1)} %get-tuple-element.51, f32[512]{0:T(512)S(1)} %get-tuple-element.52), kind=kLoop, calls=%fused_computation.57 | loop fusion | flops 4718592 | bytes 1054720 | tf_op jit(solution)/shard_map/convert.6
  21.8 168.8 %all-reduce.4.cloned.1.call-done = (bf16[32,8,1024]{0,1,2:T(8,128)(2,1)}, bf16[32,8,1024]{0,1,2:T(8,128)(2,1)}, bf16[32,8,1024]{0,1,2:T(8,128)(2,1)}, bf16[32,8,1024]{0,1,2:T(8,128)(2,1)}) async-done(((bf16[32,8,1024]{0,1,2:T(8,128)(2,1)}, bf16[32,8,1024]{0,1,2:T(8,128)(2,1)}, bf16[32,8,1024]{0,1,2:T(8,128)(2,1)}, bf16[32,8,1024]{0,1,2:T(8,128)(2,1)}), (bf16[32,8,1024]{0,1,2:T(8,128)(2,1)}, ...) | async-done | bytes 2097168 | tf_op jit(solution)/shard_map/psum | solution.py:14
  190.6 4.1 %broadcast_multiply_fusion.3 = (bf16[32,8,1024]{0,1,2:T(8,128)(2,1)S(1)}, bf16[32,8,1024]{0,1,2:T(8,128)(2,1)S(1)}, bf16[32,8,1024]{0,1,2:T(8,128)(2,1)S(1)}, bf16[32,8,1024]{0,1,2:T(8,128)(2,1)S(1)}) fusion(bf16[32,8,1024]{0,1,2:T(8,128)(2,1)} %get-tuple-element.12, bf16[8]{0:T(256)(128)(2,1)S(1)} %convert_element_type.33, ...), kind=kLoop, calls=%fused_computation.63 | loop fusion | flops 1048576 | bytes 4194320 | tf_op jit(solution)/shard_map/mul | solution.py:42
  194.9 4.3 %fusion.36 = f32[512,64,32]{1,2,0:T(8,128)} fusion(bf16[32,8,1024]{0,1,2:T(8,128)(2,1)S(1)} %copy.28, bf16[32,8,512]{0,1,2:T(8,128)(2,1)S(1)} %get-tuple-element.26, bf16[32,8,512]{0,1,2:T(8,128)(2,1)S(1)} %get-tuple-element.25), kind=kOutput, calls=%fused_computation.71 | convolution fusion | flops 17825792 | bytes 7340032 | tf_op jit(solution)/shard_map/swf,rwf->srf/dot_general | solution.py:47
  199.2 4.3 %fusion.44 = f32[512,64,32]{1,2,0:T(8,128)} fusion(bf16[32,8,1024]{0,1,2:T(8,128)(2,1)S(1)} %copy.28, bf16[32,8,512]{0,1,2:T(8,128)(2,1)S(1)} %get-tuple-element.26, bf16[32,8,512]{0,1,2:T(8,128)(2,1)S(1)} %get-tuple-element.25), kind=kOutput, calls=%fused_computation.79 | convolution fusion | flops 17825792 | bytes 7340032 | tf_op jit(solution)/shard_map/swf,rwf->srf/dot_general | solution.py:44
  203.5 4.3 %fusion.34 = f32[512,64,32]{1,2,0:T(8,128)} fusion(bf16[32,8,1024]{0,1,2:T(8,128)(2,1)S(1)} %copy.28, bf16[32,8,512]{0,1,2:T(8,128)(2,1)S(1)} %get-tuple-element.55, bf16[32,8,512]{0,1,2:T(8,128)(2,1)S(1)} %get-tuple-element.56), kind=kOutput, calls=%fused_computation.69 | convolution fusion | flops 17825792 | bytes 7340032 | tf_op jit(solution)/shard_map/swf,rwf->srf/dot_general | solution.py:47
  207.8 4.3 %fusion.42 = f32[512,64,32]{1,2,0:T(8,128)} fusion(bf16[32,8,1024]{0,1,2:T(8,128)(2,1)S(1)} %copy.28, bf16[32,8,512]{0,1,2:T(8,128)(2,1)S(1)} %get-tuple-element.55, bf16[32,8,512]{0,1,2:T(8,128)(2,1)S(1)} %get-tuple-element.56), kind=kOutput, calls=%fused_computation.77 | convolution fusion | flops 17825792 | bytes 7340032 | tf_op jit(solution)/shard_map/swf,rwf->srf/dot_general | solution.py:44
  212.3 4.3 %fusion.40 = f32[512,64,32]{1,2,0:T(8,128)} fusion(bf16[32,8,1024]{0,1,2:T(8,128)(2,1)S(1)} %copy.28, bf16[32,8,512]{0,1,2:T(8,128)(2,1)S(1)} %get-tuple-element.22, bf16[32,8,512]{0,1,2:T(8,128)(2,1)S(1)} %get-tuple-element.21), kind=kOutput, calls=%fused_computation.75 | convolution fusion | flops 17825792 | bytes 7340032 | tf_op jit(solution)/shard_map/swf,rwf->srf/dot_general | solution.py:47
  216.6 4.3 %fusion.48 = f32[512,64,32]{1,2,0:T(8,128)} fusion(bf16[32,8,1024]{0,1,2:T(8,128)(2,1)S(1)} %copy.28, bf16[32,8,512]{0,1,2:T(8,128)(2,1)S(1)} %get-tuple-element.22, bf16[32,8,512]{0,1,2:T(8,128)(2,1)S(1)} %get-tuple-element.21), kind=kOutput, calls=%fused_computation.83 | convolution fusion | flops 17825792 | bytes 7340032 | tf_op jit(solution)/shard_map/swf,rwf->srf/dot_general | solution.py:44
  220.9 4.3 %fusion.38 = f32[512,64,32]{1,2,0:T(8,128)} fusion(bf16[32,8,1024]{0,1,2:T(8,128)(2,1)S(1)} %copy.28, bf16[32,8,512]{0,1,2:T(8,128)(2,1)S(1)} %get-tuple-element.53, bf16[32,8,512]{0,1,2:T(8,128)(2,1)S(1)} %get-tuple-element.54), kind=kOutput, calls=%fused_computation.73 | convolution fusion | flops 17825792 | bytes 7340032 | tf_op jit(solution)/shard_map/swf,rwf->srf/dot_general | solution.py:47
  225.2 4.3 %fusion.46 = f32[512,64,32]{1,2,0:T(8,128)} fusion(bf16[32,8,1024]{0,1,2:T(8,128)(2,1)S(1)} %copy.28, bf16[32,8,512]{0,1,2:T(8,128)(2,1)S(1)} %get-tuple-element.53, bf16[32,8,512]{0,1,2:T(8,128)(2,1)S(1)} %get-tuple-element.54), kind=kOutput, calls=%fused_computation.81 | convolution fusion | flops 17825792 | bytes 7340032 | tf_op jit(solution)/shard_map/swf,rwf->srf/dot_general | solution.py:44
  229.4 7.7 %copy.38 = f32[512,64,32]{0,2,1:T(8,128)} copy(f32[512,64,32]{1,2,0:T(8,128)} %fusion.36) | data formatting | bytes 8388608 | tf_op jit(solution)/shard_map/swf,rwf->srf/dot_general | solution.py:47
  237.2 7.7 %copy.37 = f32[512,64,32]{0,2,1:T(8,128)} copy(f32[512,64,32]{1,2,0:T(8,128)} %fusion.44) | data formatting | bytes 8388608 | tf_op jit(solution)/shard_map/swf,rwf->srf/dot_general | solution.py:44
  244.9 7.6 %copy.41 = f32[512,64,32]{0,2,1:T(8,128)} copy(f32[512,64,32]{1,2,0:T(8,128)} %fusion.34) | data formatting | bytes 8388608 | tf_op jit(solution)/shard_map/swf,rwf->srf/dot_general | solution.py:47
  252.5 7.8 %copy.40 = f32[512,64,32]{0,2,1:T(8,128)} copy(f32[512,64,32]{1,2,0:T(8,128)} %fusion.42) | data formatting | bytes 8388608 | tf_op jit(solution)/shard_map/swf,rwf->srf/dot_general | solution.py:44
  260.3 7.8 %copy.32 = f32[512,64,32]{0,2,1:T(8,128)} copy(f32[512,64,32]{1,2,0:T(8,128)} %fusion.40) | data formatting | bytes 8388608 | tf_op jit(solution)/shard_map/swf,rwf->srf/dot_general | solution.py:47
  268.1 7.7 %copy.30 = f32[512,64,32]{0,2,1:T(8,128)} copy(f32[512,64,32]{1,2,0:T(8,128)} %fusion.48) | data formatting | bytes 8388608 | tf_op jit(solution)/shard_map/swf,rwf->srf/dot_general | solution.py:44
  275.8 7.7 %copy.35 = f32[512,64,32]{0,2,1:T(8,128)} copy(f32[512,64,32]{1,2,0:T(8,128)} %fusion.38) | data formatting | bytes 8388608 | tf_op jit(solution)/shard_map/swf,rwf->srf/dot_general | solution.py:47
  283.5 7.8 %copy.34 = f32[512,64,32]{0,2,1:T(8,128)} copy(f32[512,64,32]{1,2,0:T(8,128)} %fusion.46) | data formatting | bytes 8388608 | tf_op jit(solution)/shard_map/swf,rwf->srf/dot_general | solution.py:44
  291.3 4.4 %fusion.3 = (bf16[32,32,512]{2,1,0:T(8,128)(2,1)S(1)}, bf16[32,32,512]{2,1,0:T(8,128)(2,1)S(1)}) fusion(f32[64,32,512]{2,1,0:T(8,128)} %bitcast.40, f32[64,32,512]{2,1,0:T(8,128)} %bitcast.42), kind=kLoop, calls=%fused_computation.8 | loop fusion | flops 2097152 | bytes 10485760 | tf_op jit(solution)/shard_map/convert.2
  298.5 1.4 abs_reduce_fusion.1
  299.9 2.6 abs_reduce_fusion
  302.5 1.6 copy-done.3
  305.4 2.6 abs_reduce_fusion.3
  308.0 1.6 copy-done.1
  310.9 2.6 abs_reduce_fusion.2
  313.5 32.1 %all-reduce = (f32[32]{0:T(128)S(1)}, f32[32]{0:T(128)S(1)}, f32[32]{0:T(128)S(1)}, f32[32]{0:T(128)S(1)}) all-reduce(f32[32]{0:T(128)S(1)} %get-tuple-element.43, f32[32]{0:T(128)S(1)} %get-tuple-element.45, f32[32]{0:T(128)S(1)} %get-tuple-element.47, f32[32]{0:T(128)S(1)} %get-tuple-element.49), channel_id=1, replica_groups=mesh['parts'=2,'chan'=16] {'chan'}, use_global_device_ids=true, to_apply=%region_11.12 | all-reduce | flops 128 | bytes 1024 | tf_op jit(solution)/shard_map/pmax | solution.py:58
  345.6 1.9 fusion.33
  350.2 2.3 pad_maximum_fusion
  (33 shorter events, 9.1 us)
Async XLA Ops:
  6.5 184.0 %all-reduce.4.cloned.1.call-start = ((), (), s32[]{:S(2)}) async-start(), calls=%async_computation | async-start | bytes 16777216 | tf_op jit(solution)/shard_map/psum | solution.py:14
  16.7 0.7 copy-start.8
  291.3 4.7 %copy-start.4 = (f32[512,64,32]{0,2,1:T(8,128)S(1)}, f32[512,64,32]{0,2,1:T(8,128)}, u32[]{:S(2)}) copy-start(f32[512,64,32]{0,2,1:T(8,128)} %copy.41) | copy-start | bytes 12582916
  291.3 5.9 %copy-start.5 = (f32[512,64,32]{0,2,1:T(8,128)S(1)}, f32[512,64,32]{0,2,1:T(8,128)}, u32[]{:S(2)}) copy-start(f32[512,64,32]{0,2,1:T(8,128)} %copy.40) | copy-start | bytes 12582916
  299.9 2.6 copy-start.2
  299.9 4.2 %copy-start.3 = (f32[512,64,32]{0,2,1:T(8,128)S(1)}, f32[512,64,32]{0,2,1:T(8,128)}, u32[]{:S(2)}) copy-start(f32[512,64,32]{0,2,1:T(8,128)} %copy.30) | copy-start | bytes 12582916
  305.4 2.6 copy-start
  305.4 4.2 %copy-start.1 = (f32[512,64,32]{0,2,1:T(8,128)S(1)}, f32[512,64,32]{0,2,1:T(8,128)}, u32[]{:S(2)}) copy-start(f32[512,64,32]{0,2,1:T(8,128)} %copy.34) | copy-start | bytes 12582916
  347.6 1.6 copy-start.7
  347.9 2.0 copy-start.6
Sparse Core Ops, SparseCore 0:
  16.8 173.7 all-reduce.3
where the time goes:
time: 360 us; the launch traced here: 359 us
  waiting for transfers between devices  169 us (47%)
  local copies, waits for them, and re-layouts  73.5 us (20%)
  matrix products  43.4 us (12%)
  blocking collectives  32.1 us (9%)
  other arithmetic  25.4 us (7%)
  between operations  16 us (4%)
    psum x1, waiting for transfers between devices, from_root(): return lax.psum(block, axis)  169 us
    pmax x1, blocking collectives, shards(): global_peak = lax.pmax(local_peak, 'chan')  32.1 us
    dot_general x4, local copies, waits for them, and re-layouts, shards(): jnp.einsum('swf,rwf->srf', stacked_src, real_rcv, preferred_element_type=...  31 us
    dot_general x4, local copies, waits for them, and re-layouts, shards(): jnp.einsum('swf,rwf->srf', stacked_src, imag_rcv, preferred_element_type=...  30.8 us
    dot_general x4, matrix products, shards(): jnp.einsum('swf,rwf->srf', stacked_src, imag_rcv, preferred_element_type=...  17.2 us
    dot_general x4, matrix products, shards(): jnp.einsum('swf,rwf->srf', stacked_src, real_rcv, preferred_element_type=...  17 us
    another operation x5, other arithmetic  12.6 us
    unnamed x19, local copies, waits for them, and re-layouts  9.71 us
  transfers between devices with their start and end apart: 1, of which 1 were waited for; matrix products, arithmetic and copies ran while one was open for 1% of the time, Pallas kernels for 0%

commit v1 on v0

v1 whole, which is shorter than its diff:
```python
import functools
import math

import jax
import jax.numpy as jnp
import ml_dtypes
import numpy as np
from jax import lax
from jax.experimental import pallas as pl
from jax.experimental.pallas import tpu as pltpu
from jax.sharding import PartitionSpec as P

SOURCE = 32
LAGS = 512
GROUP = 16
VMEM_LIMIT = 56 * 1024 * 1024


def build_table(bins, lags):
    freq = np.arange(bins)[:, None]
    shifted = np.arange(lags)[None, :] - lags // 2
    theta = np.remainder(freq * shifted, 2 * bins) * (2.0 * math.pi / (2 * bins))
    weight = np.where(freq == 0, 1.0, 2.0) / (2 * bins)
    table = np.concatenate([weight * np.cos(theta), -weight * np.sin(theta)], axis=0)
    return table.astype(np.float32).astype(ml_dtypes.bfloat16)


def at_chan(index):
    return {"chan": index}


def greet_all(n, me):
    barrier = pltpu.get_barrier_semaphore()
    for off in range(1, n):
        pl.semaphore_signal(
            barrier, inc=1, device_id=at_chan(lax.rem(me + off, n)),
            device_id_type=pl.DeviceIdType.MESH,
        )
    pl.semaphore_wait(barrier, n - 1)


def gather_kernel(n, x_ref, blocks_ref, mask_ref, out_ref, cand, held, a_send, a_recv, g_send, g_recv):
    me = lax.axis_index("chan")
    z = me // 4
    y = lax.rem(me // 2, 2)
    core = lax.rem(me, 2)
    per = x_ref.shape[0] // n
    greet_all(n, me)

    def a_copy(off):
        to = lax.rem(me + off, n)
        return pltpu.make_async_remote_copy(
            src_ref=x_ref.at[pl.ds(to * per, per)], dst_ref=cand.at[me],
            send_sem=a_send.at[off], recv_sem=a_recv.at[me],
            device_id=at_chan(to), device_id_type=pl.DeviceIdType.MESH,
        )

    for off in range(1, n):
        a_copy(off).start()
    cand[me] = x_ref[pl.ds(me * per, per)]
    for off in range(1, n):
        frm = lax.rem(me + n - off, n)
        pltpu.make_async_remote_copy(
            src_ref=cand.at[frm], dst_ref=cand.at[frm],
            send_sem=a_send.at[off], recv_sem=a_recv.at[frm],
            device_id=at_chan(frm), device_id_type=pl.DeviceIdType.MESH,
        ).wait_recv()
    mask = mask_ref[...]
    for k in range(4):
        b = blocks_ref[k // 2, k % 2]
        held[pl.ds(me * per, per), SOURCE * k:SOURCE * (k + 1), :] = cand[b] * mask

    def index(zz, yy, cc):
        return (zz * 2 + yy) * 2 + cc

    def g_copy(piece, to, lane):
        ref = held.at[pl.ds(piece * per, per)]
        return pltpu.make_async_remote_copy(
            src_ref=ref, dst_ref=ref, send_sem=g_send.at[lane, piece],
            recv_sem=g_recv.at[piece], device_id=at_chan(to),
            device_id_type=pl.DeviceIdType.MESH,
        )

    y_mate = index(z, 1 - y, core)
    c_mate = index(z, y, 1 - core)
    up = lax.rem(me + 4, n)
    down = lax.rem(me + n - 4, n)

    sent = []

    def send(cond, copy):
        sent.append((cond, copy))
        if cond is None:
            copy.start()
        else:
            pl.when(cond)(copy.start)

    def arrive(cond, piece):
        copy = g_copy(piece, c_mate, 0)
        if cond is None:
            copy.wait_recv()
        else:
            pl.when(cond)(copy.wait_recv)

    send(z < 3, g_copy(me, up, 0))
    send(z > 0, g_copy(me, down, 1))
    send(None, g_copy(me, y_mate, 2))
    send(None, g_copy(me, c_mate, 3))

    def y_arrived(cond, zz):
        piece = index(zz, 1 - y, core)
        arrive(cond, piece)
        send(cond, g_copy(piece, c_mate, 3))

    def clamp(zz):
        return jnp.clip(zz, 0, 3)

    for d in range(1, 4):
        low, low_z = z >= d, clamp(z - d)
        high, high_z = z + d <= 3, clamp(z + d)
        for cond, zz, onward, to, lane in (
            (low, low_z, jnp.logical_and(low, z < 3), up, 0),
            (high, high_z, jnp.logical_and(high, z > 0), down, 1),
        ):
            piece = index(zz, y, core)
            arrive(cond, piece)
            send(onward, g_copy(piece, to, lane))
            send(cond, g_copy(piece, y_mate, 2))
            send(cond, g_copy(piece, c_mate, 3))
        if d == 1:
            y_arrived(None, z)
        else:
            y_arrived(z >= d - 1, clamp(z - d + 1))
            y_arrived(z + d - 1 <= 3, clamp(z + d - 1))
    y_arrived(z >= 3, clamp(z - 3))
    y_arrived(z <= 0, clamp(z + 3))
    for zz in range(4):
        for yy in range(2):
            arrive(None, index(zz, yy, 1 - core))
    for off in range(1, n):
        a_copy(off).wait_send()
    for cond, copy in sent:
        if cond is None:
            copy.wait_send()
        else:
            pl.when(cond)(copy.wait_send)
    out_ref[...] = held[...]


def gather_sources(n, x, blocks, mask):
    groups, channels, depth = x.shape
    vmem = pl.BlockSpec(memory_space=pltpu.VMEM)
    return pl.pallas_call(
        functools.partial(gather_kernel, n),
        out_shape=jax.ShapeDtypeStruct((groups, 4 * SOURCE, depth), x.dtype),
        in_specs=[vmem, pl.BlockSpec(memory_space=pltpu.SMEM), vmem],
        out_specs=vmem,
        scratch_shapes=[
            pltpu.VMEM((n, groups // n, channels, depth), x.dtype),
            pltpu.VMEM((groups, 4 * SOURCE, depth), x.dtype),
            pltpu.SemaphoreType.DMA((n,)),
            pltpu.SemaphoreType.DMA((n,)),
            pltpu.SemaphoreType.DMA((4, n)),
            pltpu.SemaphoreType.DMA((n,)),
        ],
        compiler_params=pltpu.CompilerParams(
            collective_id=0, has_side_effects=True, vmem_limit_bytes=VMEM_LIMIT
        ),
        name="gather_sources",
    )(x, blocks, mask)


def correlate_kernel(s_ref, x_ref, table_ref, trace_ref, peak_ref, cross, pk):
    groups, rows, depth = s_ref.shape
    receivers = x_ref.shape[1]
    half = depth // 2
    diag = lax.rem(lax.broadcasted_iota(jnp.int32, (GROUP, depth), 1), GROUP) == (
        lax.broadcasted_iota(jnp.int32, (GROUP, depth), 0)
    )

    def first(g, carry):
        v = x_ref[g].astype(jnp.float32)
        turned = jnp.concatenate([v[:, half:], -v[:, :half]], axis=1)
        both = jnp.stack([v, turned], axis=1)
        spread = jnp.where(diag[None, None], both[:, :, None, :], 0.0).astype(jnp.bfloat16)
        spread = spread.reshape(receivers * 2 * GROUP, depth)
        out = lax.dot_general(
            spread, s_ref[g], (((1,), (1,)), ((), ())), preferred_element_type=jnp.float32
        ).astype(jnp.bfloat16)
        where = pl.ds(pl.multiple_of(g * GROUP, GROUP), GROUP)
        cross[:, :, where, :] = out.reshape(receivers, 2, GROUP, rows)
        return carry

    lax.fori_loop(0, groups, first, 0)

    pk[...] = jnp.zeros_like(pk)
    step = 4
    lanes = pk.shape[1]

    def second(i, carry):
        parts = [
            cross[i * step + q].reshape(2 * groups * GROUP, rows).T for q in range(step)
        ]
        out = jnp.dot(
            jnp.concatenate(parts, axis=0), table_ref[...], preferred_element_type=jnp.float32
        )
        best = pk[...]
        for q in range(step):
            piece = out[q * rows:(q + 1) * rows]
            for c in range(LAGS // lanes):
                cols = piece[:, c * lanes:(c + 1) * lanes]
                trace_ref[c, pl.ds(i * step + q, rows, stride=receivers), :] = cols
                best = jnp.maximum(best, jnp.abs(cols))
        pk[...] = best
        return carry

    lax.fori_loop(0, receivers // step, second, 0)
    peak_ref[...] = jnp.broadcast_to(jnp.max(pk[...].T, axis=0, keepdims=True), peak_ref.shape)


def correlate(sources, x, table):
    groups, rows, depth = sources.shape
    receivers = x.shape[1]
    vmem = pl.BlockSpec(memory_space=pltpu.VMEM)
    return pl.pallas_call(
        correlate_kernel,
        out_shape=(
            jax.ShapeDtypeStruct((LAGS // 128, rows * receivers, 128), jnp.float32),
            jax.ShapeDtypeStruct((8, rows), jnp.float32),
        ),
        in_specs=[vmem] * 3,
        out_specs=(vmem, vmem),
        scratch_shapes=[
            pltpu.VMEM((receivers, 2, groups * GROUP, rows), jnp.bfloat16),
            pltpu.VMEM((rows, 128), jnp.float32),
        ],
        compiler_params=pltpu.CompilerParams(vmem_limit_bytes=VMEM_LIMIT),
        name="correlate",
    )(sources, x, table)


def peak_kernel(n, peak_ref, out_ref, slots, send_sem, recv_sem):
    me = lax.axis_index("chan")
    greet_all(n, me)

    def copy(off):
        return pltpu.make_async_remote_copy(
            src_ref=peak_ref, dst_ref=slots.at[me], send_sem=send_sem.at[off],
            recv_sem=recv_sem.at[me], device_id=at_chan(lax.rem(me + off, n)),
            device_id_type=pl.DeviceIdType.MESH,
        )

    for off in range(1, n):
        copy(off).start()
    slots[me] = peak_ref[...]
    for off in range(1, n):
        frm = lax.rem(me + n - off, n)
        pltpu.make_async_remote_copy(
            src_ref=slots.at[frm], dst_ref=slots.at[frm], send_sem=send_sem.at[off],
            recv_sem=recv_sem.at[frm], device_id=at_chan(frm),
            device_id_type=pl.DeviceIdType.MESH,
        ).wait_recv()
    out_ref[...] = jnp.max(slots[...], axis=0)
    for off in range(1, n):
        copy(off).wait_send()


def share_peak(n, peak):
    vmem = pl.BlockSpec(memory_space=pltpu.VMEM)
    return pl.pallas_call(
        functools.partial(peak_kernel, n),
        out_shape=jax.ShapeDtypeStruct(peak.shape, peak.dtype),
        in_specs=[vmem],
        out_specs=vmem,
        scratch_shapes=[
            pltpu.VMEM((n,) + peak.shape, peak.dtype),
            pltpu.SemaphoreType.DMA((n,)),
            pltpu.SemaphoreType.DMA((n,)),
        ],
        compiler_params=pltpu.CompilerParams(collective_id=1, has_side_effects=True),
        name="share_peak",
    )(peak)


def scale_kernel(block, receivers, peak_ref, trace_ref, out_ref):
    i = pl.program_id(0)
    for q in range(block):
        peak = jnp.full((1, 128), peak_ref[0, i * block + q], jnp.float32)
        inverse = 1.0 / (peak + 1e-06)
        here = slice(q * receivers, (q + 1) * receivers)
        for c in range(LAGS // 128):
            cols = slice(c * 128, (c + 1) * 128)
            out_ref[here, cols] = (trace_ref[c, here, :] * inverse).astype(jnp.bfloat16)


def scale(trace, peak, receivers):
    block = 16
    total = trace.shape[1]
    steps = total // (block * receivers)
    return pl.pallas_call(
        functools.partial(scale_kernel, block, receivers),
        out_shape=jax.ShapeDtypeStruct((total, LAGS), jnp.bfloat16),
        grid=(steps,),
        in_specs=[
            pl.BlockSpec(memory_space=pltpu.SMEM),
            pl.BlockSpec((LAGS // 128, block * receivers, 128), lambda i: (0, i, 0)),
        ],
        out_specs=pl.BlockSpec((block * receivers, LAGS), lambda i: (i, 0)),
        compiler_params=pltpu.CompilerParams(vmem_limit_bytes=VMEM_LIMIT),
        name="scale",
    )(peak, trace)


def shards(n, spectra, source_blocks, window_valid):
    receivers, windows, width = spectra.shape
    bins = width // 2
    groups = bins // GROUP
    num_steps = source_blocks.shape[0]
    x = spectra.reshape(receivers, windows, 2, groups, GROUP).transpose(3, 0, 2, 1, 4)
    x = x.reshape(groups, receivers, 2 * windows * GROUP)
    mask = jnp.tile(jnp.repeat(window_valid.astype(jnp.bfloat16), GROUP), 2)[None, :]
    table = jnp.asarray(build_table(bins, LAGS))
    if n == 16:
        sources = gather_sources(n, x, source_blocks, mask)
    else:
        roots = source_blocks.reshape(-1) // (receivers // SOURCE)
        mine = (roots == lax.axis_index("chan"))[None, :, None, None]
        picked = jnp.where(mine, (x * mask)[:, None], jnp.zeros((), x.dtype))
        sources = lax.psum(picked.reshape(groups, -1, x.shape[2]), "chan")
    trace, peak = correlate(sources, x, table)
    peak = share_peak(n, peak) if n == 16 else lax.pmax(peak, "chan")
    out = scale(trace, peak, receivers)
    return out.reshape(num_steps, 2, SOURCE, receivers, LAGS)


def solution(mesh):
    placed = (P(("parts", "chan"), None, None), P("parts", None), P("parts"))
    return jax.shard_map(
        functools.partial(shards, mesh.shape["chan"]),
        mesh=mesh,
        in_specs=placed,
        out_specs=P(None, None, None, ("parts", "chan"), None),
        check_vma=False,
    )
```

time: 360 us -> 94.7 us (0.26)
  waiting for transfers between devices: 169 us -> 0 us
  Pallas kernels: 0 us -> 86.4 us
  local copies, waits for them, and re-layouts: 73.5 us -> 7.17 us
  matrix products: 43.4 us -> 0 us
  blocking collectives: 32.1 us -> 0 us
  other arithmetic: 25.4 us -> 0.66 us
  between operations: 16 us -> 0.03 us
    psum x1 -> x0, waiting for transfers between devices: 169 us -> none  [from_root(): return lax.psum(block, axis)]
    pallas_call x0 -> x4, Pallas kernels: none -> 86.4 us  [the longest x1 41.2 us: gather_sources(): pl.pallas_call(functools.partial(gather_kernel, n), out_shape=jax.ShapeDt...]
    dot_general x8 -> x0, local copies, waits for them, and re-layouts: 61.8 us -> none  [the longest x4 31 us: shards(): jnp.einsum('swf,rwf->srf', stacked_src, real_rcv, preferred_element_type=...]
    dot_general x12 -> x0, matrix products: 43.4 us -> none  [the longest x4 17.2 us: shards(): jnp.einsum('swf,rwf->srf', stacked_src, imag_rcv, preferred_element_type=...]
    pmax x1 -> x0, blocking collectives: 32.1 us -> none  [shards(): global_peak = lax.pmax(local_peak, 'chan')]
    another operation x10 -> x0, other arithmetic: 17.9 us -> none
    unnamed x19 -> x3, local copies, waits for them, and re-layouts: 9.71 us -> 3.32 us
    mul x1 -> x0, other arithmetic: 4.08 us -> none  [shards(): masked = source * window_mask]
  transfers between devices with their start and end apart: 1 -> 0, of which waited for: 1 -> 0; matrix products, arithmetic and copies ran while one was open for 1% -> 0% of each run, Pallas kernels for 0% -> 0%
where the time goes in v1:
time: 94.7 us; the launch traced here: 94.3 us
  Pallas kernels  86.4 us (91%)
  local copies, waits for them, and re-layouts  7.17 us (8%)
    pallas_call x1, Pallas kernels, gather_sources(): pl.pallas_call(functools.partial(gather_kernel, n), out_shape=jax.ShapeDt...  41.2 us
    pallas_call x1, Pallas kernels, correlate(): pl.pallas_call(correlate_kernel, out_shape=(jax.ShapeDtypeStruct((LAGS //...  29.3 us
    pallas_call x1, Pallas kernels, share_peak(): pl.pallas_call(functools.partial(peak_kernel, n), out_shape=jax.ShapeDtyp...  7.98 us
    pallas_call x1, Pallas kernels, scale(): pl.pallas_call(functools.partial(scale_kernel, block, receivers), out_sha...  7.91 us
    unnamed x3, local copies, waits for them, and re-layouts  3.32 us
    transpose x1, local copies, waits for them, and re-layouts, shards(): spectra.reshape(receivers, windows, 2, groups, GROUP)  2.19 us

profile of v1, /device:TPU:0, one launch (start us, length us, event | category | flops | bytes accessed | tf_op | source)
XLA Modules:
  0.0 94.3 jit_solution(14781001790866639961)
XLA Ops:
  0.0 0.7 convert_element_type.3
  0.7 0.1 broadcast_in_dim.3
  0.7 0.1 tile.7
  0.8 0.6 copy.12
  1.4 2.7 %copy.6 = bf16[32,8,1024]{0,2,1:T(8,128)(2,1)} copy(bf16[32,8,1024]{2,1,0:T(8,128)(2,1)} %param.4) | data formatting | bytes 1048576 | tf_op args[0]
  4.1 2.2 %copy.7 = bf16[32,32,2,8,16]{1,4,3,2,0:T(8,128)(2,1)S(1)} copy(bf16[32,32,2,8,16]{1,4,0,2,3:T(8,128)(2,1)} %bitcast.12) | data formatting | bytes 1048576 | tf_op jit(solution)/shard_map/transpose | solution.py:319
  6.3 1.5 %copy.8.x_ref = bf16[32,32,256]{2,1,0:T(8,128)(2,1)} copy(bf16[32,32,256]{1,2,0:T(8,128)(2,1)S(1)} %bitcast.11) | data formatting | bytes 1048576 | tf_op jit(solution)/shard_map/reshape | solution.py:320
  7.8 41.2 %gather_sources.1.s_ref = bf16[32,128,256]{2,1,0:T(8,128)(2,1)} custom-call(bf16[32,32,256]{2,1,0:T(8,128)(2,1)} %copy.8.x_ref, s32[2,2]{1,0:T(2,128)} %blocks_ref.1, bf16[1,256]{1,0:T(2,128)(2,1)} %bitcast.13), custom_call_target="tpu_custom_call" | custom-call | tf_op jit(solution)/shard_map/gather_sources/pallas_call | solution.py:153
  49.1 29.3 %correlate.1 = (f32[4,4096,128]{2,1,0:T(8,128)}, f32[8,128]{1,0:T(8,128)}) custom-call(bf16[32,128,256]{2,1,0:T(8,128)(2,1)} %gather_sources.1.s_ref, bf16[32,32,256]{2,1,0:T(8,128)(2,1)} %copy.8.x_ref, bf16[1024,512]{1,0:T(8,128)(2,1)} %constant.2.clone.table_ref), custom_call_target="tpu_custom_call" | custom-call | tf_op jit(solution)/shard_map/correlate/pallas_call | solution.py:225
  78.4 8.0 %share_peak.1.peak_ref = f32[8,128]{1,0:T(8,128)} custom-call(f32[8,128]{1,0:T(8,128)} %get-tuple-element.7.peak_ref), custom_call_target="tpu_custom_call" | custom-call | tf_op jit(solution)/shard_map/share_peak/pallas_call | solution.py:270
  86.4 7.9 %scale.1 = bf16[4096,512]{1,0:T(8,128)(2,1)} custom-call(f32[8,128]{1,0:T(8,128)} %share_peak.1.peak_ref, f32[4,4096,128]{2,1,0:T(8,128)} %get-tuple-element.8.trace_ref), custom_call_target="tpu_custom_call" | custom-call | tf_op jit(solution)/shard_map/scale/pallas_call | solution.py:300
  (1 shorter events, 0.0 us)

commit v2 on v1

v2 whole, which is shorter than its diff:
```python
import functools
import math

import jax
import jax.numpy as jnp
import ml_dtypes
import numpy as np
from jax import lax
from jax.experimental import pallas as pl
from jax.experimental.pallas import tpu as pltpu
from jax.sharding import PartitionSpec as P

SOURCE = 32
LAGS = 512
GROUP = 16
VMEM_LIMIT = 56 * 1024 * 1024


def build_table(bins, lags):
    freq = np.arange(bins)[:, None]
    shifted = np.arange(lags)[None, :] - lags // 2
    theta = np.remainder(freq * shifted, 2 * bins) * (2.0 * math.pi / (2 * bins))
    weight = np.where(freq == 0, 1.0, 2.0) / (2 * bins)
    table = np.concatenate([weight * np.cos(theta), -weight * np.sin(theta)], axis=0)
    return table.astype(np.float32).astype(ml_dtypes.bfloat16)


def at_chan(index):
    return {"chan": index}


def fused_kernel(
    n, a_ref, blocks_ref, valid_ref, rows_ref, cols_ref, table_ref, out_ref,
    x, cand0, cand1, held, spread, cross, trace, stage, pk, slots, inverse,
    a_send, a_recv, g_send, g_recv, p_send, p_recv, o_sem,
):
    me = lax.axis_index("chan")
    z = me // 4
    y = lax.rem(me // 2, 2)
    core = lax.rem(me, 2)
    groups, receivers, depth = x.shape
    per = groups // n
    half = depth // 2
    rows = held.shape[1]
    mesh_ids = pl.DeviceIdType.MESH
    cand = (cand0, cand1)

    barrier = pltpu.get_barrier_semaphore()
    for off in range(1, n):
        pl.semaphore_signal(
            barrier, inc=1, device_id=at_chan(lax.rem(me + off, n)), device_id_type=mesh_ids
        )

    by_window = jnp.dot(
        rows_ref[...], a_ref[...], preferred_element_type=jnp.float32
    ).astype(jnp.bfloat16)
    windows = by_window.shape[0] // receivers
    tiles = by_window.shape[1] // half
    flat = jnp.concatenate(
        [
            jnp.concatenate(
                [
                    by_window[w * receivers:(w + 1) * receivers, t * half:(t + 1) * half]
                    for w in range(windows)
                ],
                axis=1,
            )
            for t in range(tiles)
        ],
        axis=0,
    )
    turned = jnp.dot(flat, cols_ref[...], preferred_element_type=jnp.float32).astype(jnp.bfloat16)
    high = tiles // 2
    low = groups // high
    for t in range(tiles):
        c, gh = t // high, t % high
        for gl in range(low):
            x[gh * low + gl, :, c * half:(c + 1) * half] = turned[
                t * receivers:(t + 1) * receivers, gl * half:(gl + 1) * half
            ]

    pl.semaphore_wait(barrier, n - 1)

    def a_copy(h, off):
        to = lax.rem(me + off, n)
        return pltpu.make_async_remote_copy(
            src_ref=x.at[to * per + h], dst_ref=cand[h].at[me],
            send_sem=a_send.at[h, off], recv_sem=a_recv.at[h, me],
            device_id=at_chan(to), device_id_type=mesh_ids,
        )

    for h in range(per):
        for off in range(1, n):
            a_copy(h, off).start()
    for h in range(per):
        cand[h][me] = x[me * per + h]

    diag = lax.rem(lax.broadcasted_iota(jnp.int32, (GROUP, depth), 1), GROUP) == (
        lax.broadcasted_iota(jnp.int32, (GROUP, depth), 0)
    )

    def widen(g, carry):
        v = x[g].astype(jnp.float32)
        rotated = jnp.concatenate([v[:, half:], -v[:, :half]], axis=1)
        both = jnp.stack([v, rotated], axis=1)
        wide = jnp.where(diag[None, None], both[:, :, None, :], 0.0).astype(jnp.bfloat16)
        spread[g] = wide.reshape(receivers * 2 * GROUP, depth)
        return carry

    lax.fori_loop(0, groups, widen, 0)

    window = lax.rem(lax.broadcasted_iota(jnp.int32, (1, depth), 1), half) // GROUP
    mask = jnp.zeros((1, depth), jnp.float32)
    for w in range(windows):
        mask = jnp.where(window == w, valid_ref[w].astype(jnp.float32), mask)
    mask = mask.astype(jnp.bfloat16)

    def index(zz, yy, cc):
        return (zz * 2 + yy) * 2 + cc

    def g_copy(h, piece, to, lane):
        ref = held.at[piece * per + h]
        return pltpu.make_async_remote_copy(
            src_ref=ref, dst_ref=ref, send_sem=g_send.at[h, lane, piece],
            recv_sem=g_recv.at[h, piece], device_id=at_chan(to), device_id_type=mesh_ids,
        )

    y_mate = index(z, 1 - y, core)
    c_mate = index(z, y, 1 - core)
    up = lax.rem(me + 4, n)
    down = lax.rem(me + n - 4, n)
    sent = []

    def guarded(cond, action):
        if cond is None:
            action()
        else:
            pl.when(cond)(action)

    def send(cond, copy):
        sent.append((cond, copy))
        guarded(cond, copy.start)

    def arrive(cond, h, piece):
        guarded(cond, g_copy(h, piece, c_mate, 0).wait_recv)

    def first(piece):
        def body(h, carry):
            g = piece * per + h
            out = lax.dot_general(
                spread[g], held[g], (((1,), (1,)), ((), ())), preferred_element_type=jnp.float32
            ).astype(jnp.bfloat16)
            where = pl.ds(pl.multiple_of(g * GROUP, GROUP), GROUP)
            cross[:, :, where, :] = out.reshape(receivers, 2, GROUP, rows)
            return carry

        lax.fori_loop(0, per, body, 0)

    for h in range(per):
        for off in range(1, n):
            frm = lax.rem(me + n - off, n)
            pltpu.make_async_remote_copy(
                src_ref=cand[h].at[frm], dst_ref=cand[h].at[frm],
                send_sem=a_send.at[h, off], recv_sem=a_recv.at[h, frm],
                device_id=at_chan(frm), device_id_type=mesh_ids,
            ).wait_recv()
        for k in range(4):
            b = blocks_ref[k // 2, k % 2]
            held[me * per + h, SOURCE * k:SOURCE * (k + 1), :] = cand[h][b] * mask
        send(z < 3, g_copy(h, me, up, 0))
        send(z > 0, g_copy(h, me, down, 1))
        send(None, g_copy(h, me, y_mate, 2))
        send(None, g_copy(h, me, c_mate, 3))

    def clamp(zz):
        return jnp.clip(zz, 0, 3)

    ready = [(None, me)]

    def y_arrived(cond, zz):
        piece = index(zz, 1 - y, core)
        for h in range(per):
            arrive(cond, h, piece)
            send(cond, g_copy(h, piece, c_mate, 3))
        ready.append((cond, piece))

    def work():
        for cond, piece in ready:
            guarded(cond, functools.partial(first, piece))
        ready.clear()

    for d in range(1, 4):
        low_in, low_z = z >= d, clamp(z - d)
        high_in, high_z = z + d <= 3, clamp(z + d)
        ways = (
            (low_in, low_z, jnp.logical_and(low_in, z < 3), up, 0),
            (high_in, high_z, jnp.logical_and(high_in, z > 0), down, 1),
        )
        for h in range(per):
            for cond, zz, onward, to, lane in ways:
                piece = index(zz, y, core)
                arrive(cond, h, piece)
                send(onward, g_copy(h, piece, to, lane))
                send(cond, g_copy(h, piece, y_mate, 2))
                send(cond, g_copy(h, piece, c_mate, 3))
        if d == 1:
            y_arrived(None, z)
        else:
            y_arrived(z >= d - 1, clamp(z - d + 1))
            y_arrived(z + d - 1 <= 3, clamp(z + d - 1))
        work()
        for cond, zz, _, _, _ in ways:
            ready.append((cond, index(zz, y, core)))
    y_arrived(z >= 3, clamp(z - 3))
    y_arrived(z <= 0, clamp(z + 3))
    work()

    def others(i, carry):
        piece = index(i // 2, lax.rem(i, 2), 1 - core)
        for h in range(per):
            arrive(None, h, piece)
        first(piece)
        return carry

    lax.fori_loop(0, n // 2, others, 0)

    pk[...] = jnp.zeros_like(pk)
    step = 4
    lanes = pk.shape[1]

    def second(i, carry):
        parts = [cross[i * step + q].reshape(2 * groups * GROUP, rows).T for q in range(step)]
        out = jnp.dot(
            jnp.concatenate(parts, axis=0), table_ref[...], preferred_element_type=jnp.float32
        )
        best = pk[...]
        for q in range(step):
            piece = out[q * rows:(q + 1) * rows]
            for c in range(LAGS // lanes):
                part = piece[:, c * lanes:(c + 1) * lanes]
                trace[c, pl.ds(i * step + q, rows, stride=receivers), :] = part
                best = jnp.maximum(best, jnp.abs(part))
        pk[...] = best
        return carry

    lax.fori_loop(0, receivers // step, second, 0)

    own = jnp.max(pk[...].T, axis=0, keepdims=True)
    slots[me] = jnp.broadcast_to(own, slots.shape[1:])

    def p_copy(off):
        return pltpu.make_async_remote_copy(
            src_ref=slots.at[me], dst_ref=slots.at[me], send_sem=p_send.at[off],
            recv_sem=p_recv.at[me], device_id=at_chan(lax.rem(me + off, n)),
            device_id_type=mesh_ids,
        )

    for off in range(1, n):
        p_copy(off).start()
    for h in range(per):
        for off in range(1, n):
            a_copy(h, off).wait_send()
    for cond, copy in sent:
        guarded(cond, copy.wait_send)
    for off in range(1, n):
        frm = lax.rem(me + n - off, n)
        pltpu.make_async_remote_copy(
            src_ref=slots.at[frm], dst_ref=slots.at[frm], send_sem=p_send.at[off],
            recv_sem=p_recv.at[frm], device_id=at_chan(frm), device_id_type=mesh_ids,
        ).wait_recv()
    top = jnp.max(jnp.max(slots[...], axis=0), axis=0, keepdims=True)
    inverse[...] = 1.0 / (jnp.broadcast_to(top, inverse.shape).T + 1e-06)

    block = rows // o_sem.shape[0]
    size = block * receivers

    def o_copy(i):
        here = pl.ds(pl.multiple_of(i * size, size), size)
        return pltpu.make_async_copy(stage.at[here], out_ref.at[here], o_sem.at[i])

    def finish(i, carry):
        for q in range(block):
            row = i * block + q
            factor = inverse[pl.ds(row, 1), :]
            here = pl.ds(pl.multiple_of(row * receivers, receivers), receivers)
            for c in range(LAGS // lanes):
                stage[here, c * lanes:(c + 1) * lanes] = (trace[c, here, :] * factor).astype(
                    jnp.bfloat16
                )
        o_copy(i).start()
        return carry

    lax.fori_loop(0, o_sem.shape[0], finish, 0)
    for off in range(1, n):
        p_copy(off).wait_send()
    for i in range(o_sem.shape[0]):
        o_copy(i).wait()


def reorder_tables(receivers, windows, groups):
    ch, w = np.meshgrid(np.arange(receivers), np.arange(windows), indexing="ij")
    rows = np.zeros((receivers * windows,) * 2, np.float32)
    rows[(w * receivers + ch).ravel(), (ch * windows + w).ravel()] = 1.0
    low = 128 // GROUP
    w, g, f = np.meshgrid(np.arange(windows), np.arange(low), np.arange(GROUP), indexing="ij")
    cols = np.zeros((windows * 128,) * 2, np.float32)
    cols[(w * 128 + g * GROUP + f).ravel(), (g * 128 + w * GROUP + f).ravel()] = 1.0
    return rows.astype(ml_dtypes.bfloat16), cols.astype(ml_dtypes.bfloat16)


def fused(n, spectra, blocks, valid, table):
    receivers, windows, width = spectra.shape
    groups = width // 2 // GROUP
    depth = 2 * windows * GROUP
    sources = 4 * SOURCE
    chunks = 8
    per = groups // n
    vmem = pl.BlockSpec(memory_space=pltpu.VMEM)
    smem = pl.BlockSpec(memory_space=pltpu.SMEM)
    by_row, by_col = reorder_tables(receivers, windows, groups)
    dma = pltpu.SemaphoreType.DMA
    return pl.pallas_call(
        functools.partial(fused_kernel, n),
        out_shape=jax.ShapeDtypeStruct((sources * receivers, LAGS), jnp.bfloat16),
        in_specs=[vmem, smem, smem, vmem, vmem, vmem],
        out_specs=pl.BlockSpec(memory_space=pl.ANY),
        scratch_shapes=[
            pltpu.VMEM((groups, receivers, depth), jnp.bfloat16),
            pltpu.VMEM((n, receivers, depth), jnp.bfloat16),
            pltpu.VMEM((n, receivers, depth), jnp.bfloat16),
            pltpu.VMEM((groups, sources, depth), jnp.bfloat16),
            pltpu.VMEM((groups, receivers * 2 * GROUP, depth), jnp.bfloat16),
            pltpu.VMEM((receivers, 2, groups * GROUP, sources), jnp.bfloat16),
            pltpu.VMEM((LAGS // 128, sources * receivers, 128), jnp.float32),
            pltpu.VMEM((sources * receivers, LAGS), jnp.bfloat16),
            pltpu.VMEM((sources, 128), jnp.float32),
            pltpu.VMEM((n, 8, sources), jnp.float32),
            pltpu.VMEM((sources, 128), jnp.float32),
            dma((per, n)),
            dma((per, n)),
            dma((per, 4, n)),
            dma((per, n)),
            dma((n,)),
            dma((n,)),
            dma((chunks,)),
        ],
        compiler_params=pltpu.CompilerParams(
            collective_id=0, has_side_effects=True, vmem_limit_bytes=VMEM_LIMIT
        ),
        name="fused",
    )(
        spectra.reshape(receivers * windows, width), blocks, valid,
        jnp.asarray(by_row), jnp.asarray(by_col), table,
    )


def correlate_kernel(s_ref, x_ref, table_ref, trace_ref, peak_ref, cross, pk):
    groups, rows, depth = s_ref.shape
    receivers = x_ref.shape[1]
    half = depth // 2
    diag = lax.rem(lax.broadcasted_iota(jnp.int32, (GROUP, depth), 1), GROUP) == (
        lax.broadcasted_iota(jnp.int32, (GROUP, depth), 0)
    )

    def first(g, carry):
        v = x_ref[g].astype(jnp.float32)
        turned = jnp.concatenate([v[:, half:], -v[:, :half]], axis=1)
        both = jnp.stack([v, turned], axis=1)
        spread = jnp.where(diag[None, None], both[:, :, None, :], 0.0).astype(jnp.bfloat16)
        spread = spread.reshape(receivers * 2 * GROUP, depth)
        out = lax.dot_general(
            spread, s_ref[g], (((1,), (1,)), ((), ())), preferred_element_type=jnp.float32
        ).astype(jnp.bfloat16)
        where = pl.ds(pl.multiple_of(g * GROUP, GROUP), GROUP)
        cross[:, :, where, :] = out.reshape(receivers, 2, GROUP, rows)
        return carry

    lax.fori_loop(0, groups, first, 0)

    pk[...] = jnp.zeros_like(pk)
    step = 4
    lanes = pk.shape[1]

    def second(i, carry):
        parts = [
            cross[i * step + q].reshape(2 * groups * GROUP, rows).T for q in range(step)
        ]
        out = jnp.dot(
            jnp.concatenate(parts, axis=0), table_ref[...], preferred_element_type=jnp.float32
        )
        best = pk[...]
        for q in range(step):
            piece = out[q * rows:(q + 1) * rows]
            for c in range(LAGS // lanes):
                cols = piece[:, c * lanes:(c + 1) * lanes]
                trace_ref[c, pl.ds(i * step + q, rows, stride=receivers), :] = cols
                best = jnp.maximum(best, jnp.abs(cols))
        pk[...] = best
        return carry

    lax.fori_loop(0, receivers // step, second, 0)
    peak_ref[...] = jnp.broadcast_to(jnp.max(pk[...].T, axis=0, keepdims=True), peak_ref.shape)


def correlate(sources, x, table):
    groups, rows, depth = sources.shape
    receivers = x.shape[1]
    vmem = pl.BlockSpec(memory_space=pltpu.VMEM)
    return pl.pallas_call(
        correlate_kernel,
        out_shape=(
            jax.ShapeDtypeStruct((LAGS // 128, rows * receivers, 128), jnp.float32),
            jax.ShapeDtypeStruct((8, rows), jnp.float32),
        ),
        in_specs=[vmem] * 3,
        out_specs=(vmem, vmem),
        scratch_shapes=[
            pltpu.VMEM((receivers, 2, groups * GROUP, rows), jnp.bfloat16),
            pltpu.VMEM((rows, 128), jnp.float32),
        ],
        compiler_params=pltpu.CompilerParams(vmem_limit_bytes=VMEM_LIMIT),
        name="correlate",
    )(sources, x, table)


def scale_kernel(block, receivers, peak_ref, trace_ref, out_ref):
    i = pl.program_id(0)
    for q in range(block):
        peak = jnp.full((1, 128), peak_ref[0, i * block + q], jnp.float32)
        inverse = 1.0 / (peak + 1e-06)
        here = slice(q * receivers, (q + 1) * receivers)
        for c in range(LAGS // 128):
            cols = slice(c * 128, (c + 1) * 128)
            out_ref[here, cols] = (trace_ref[c, here, :] * inverse).astype(jnp.bfloat16)


def scale(trace, peak, receivers):
    block = 16
    total = trace.shape[1]
    steps = total // (block * receivers)
    return pl.pallas_call(
        functools.partial(scale_kernel, block, receivers),
        out_shape=jax.ShapeDtypeStruct((total, LAGS), jnp.bfloat16),
        grid=(steps,),
        in_specs=[
            pl.BlockSpec(memory_space=pltpu.SMEM),
            pl.BlockSpec((LAGS // 128, block * receivers, 128), lambda i: (0, i, 0)),
        ],
        out_specs=pl.BlockSpec((block * receivers, LAGS), lambda i: (i, 0)),
        compiler_params=pltpu.CompilerParams(vmem_limit_bytes=VMEM_LIMIT),
        name="scale",
    )(peak, trace)


def shards(n, spectra, source_blocks, window_valid):
    receivers, windows, width = spectra.shape
    bins = width // 2
    groups = bins // GROUP
    num_steps = source_blocks.shape[0]
    table = jnp.asarray(build_table(bins, LAGS))
    if n == 16:
        out = fused(n, spectra, source_blocks, window_valid, table)
    else:
        x = spectra.reshape(receivers, windows, 2, groups, GROUP).transpose(3, 0, 2, 1, 4)
        x = x.reshape(groups, receivers, 2 * windows * GROUP)
        mask = jnp.tile(jnp.repeat(window_valid.astype(jnp.bfloat16), GROUP), 2)[None, :]
        roots = source_blocks.reshape(-1) // (receivers // SOURCE)
        mine = (roots == lax.axis_index("chan"))[None, :, None, None]
        picked = jnp.where(mine, (x * mask)[:, None], jnp.zeros((), x.dtype))
        sources = lax.psum(picked.reshape(groups, -1, x.shape[2]), "chan")
        trace, peak = correlate(sources, x, table)
        out = scale(trace, lax.pmax(peak, "chan"), receivers)
    return out.reshape(num_steps, 2, SOURCE, receivers, LAGS)


def solution(mesh):
    placed = (P(("parts", "chan"), None, None), P("parts", None), P("parts"))
    return jax.shard_map(
        functools.partial(shards, mesh.shape["chan"]),
        mesh=mesh,
        in_specs=placed,
        out_specs=P(None, None, None, ("parts", "chan"), None),
        check_vma=False,
    )
```

time: 94.7 us -> 67.6 us (0.71)
  Pallas kernels: 86.4 us -> 62.7 us
  local copies, waits for them, and re-layouts: 7.17 us -> 4.79 us
    pallas_call x4 -> x1, Pallas kernels: 86.4 us -> 62.7 us  [fused(): pl.pallas_call(functools.partial(fused_kernel, n), out_shape=jax.ShapeDty...]
    transpose x1 -> x0, local copies, waits for them, and re-layouts: 2.19 us -> none  [shards(): spectra.reshape(receivers, windows, 2, groups, GROUP)]
    reshape x1 -> x0, local copies, waits for them, and re-layouts: 1.5 us -> none  [shards(): x = x.reshape(groups, receivers, 2 * windows * GROUP)]
    unnamed x3 -> x1, local copies, waits for them, and re-layouts: 3.32 us -> 4.79 us
where the time goes in v2:
time: 67.6 us; the launch traced here: 67.5 us
  Pallas kernels  62.7 us (93%)
  local copies, waits for them, and re-layouts  4.79 us (7%)
    pallas_call x1, Pallas kernels, fused(): pl.pallas_call(functools.partial(fused_kernel, n), out_shape=jax.ShapeDty...  62.7 us
    unnamed x1, local copies, waits for them, and re-layouts  4.79 us

profile of v2, /device:TPU:0, one launch (start us, length us, event | category | flops | bytes accessed | tf_op | source)
XLA Modules:
  0.0 67.5 jit_solution(1570716335779392829)
XLA Ops:
  0.0 62.7 %fused.1 = bf16[4096,512]{1,0:T(8,128)(2,1)} custom-call(bf16[256,1024]{1,0:T(8,128)(2,1)} %bitcast.3, s32[2,2]{1,0:T(2,128)} %blocks_ref.1, s32[8]{0:T(128)} %valid_ref.1, bf16[256,256]{1,0:T(8,128)(2,1)} %constant.7.clone.rows_ref, bf16[1024,1024]{1,0:T(8,128)(2,1)} %constant.8.clone.cols_ref, bf16[1024,512]{1,0:T(8,128)(2,1)} %constant.6.clone.table_ref), custom_call_target="tpu_custom_call" | custom-call | tf_op jit(solution)/shard_map/fused/pallas_call | solution.py:322
  62.7 4.8 %copy.8 = bf16[2,2,32,32,512]{4,3,2,1,0:T(8,128)(2,1)} copy(bf16[2,2,32,32,512]{4,3,2,1,0:T(8,128)(2,1)} %bitcast.2) | data formatting | bytes 8388608

commit v3 on v2

--- a/solution.py
+++ b/solution.py
@@ -30,9 +30,9 @@
 
 
 def fused_kernel(
-    n, a_ref, blocks_ref, valid_ref, rows_ref, cols_ref, table_ref, out_ref,
-    x, cand0, cand1, held, spread, cross, trace, stage, pk, slots, inverse,
-    a_send, a_recv, g_send, g_recv, p_send, p_recv, o_sem,
+    n, a_ref, blocks_ref, valid_ref, rows_ref, table_hbm, out_ref,
+    table_ref, x, cand0, cand1, held, spread, cross, trace, stage, pk, slots, inverse,
+    a_send, a_recv, g_send, g_recv, p_send, p_recv, o_sem, t_sem,
 ):
     me = lax.axis_index("chan")
     z = me // 4
@@ -45,11 +45,27 @@
     mesh_ids = pl.DeviceIdType.MESH
     cand = (cand0, cand1)
 
+    table_copy = pltpu.make_async_copy(table_hbm, table_ref, t_sem)
+    table_copy.start()
     barrier = pltpu.get_barrier_semaphore()
     for off in range(1, n):
         pl.semaphore_signal(
             barrier, inc=1, device_id=at_chan(lax.rem(me + off, n)), device_id_type=mesh_ids
         )
+
+    low = half // GROUP
+    row = lax.broadcasted_iota(jnp.int32, (depth * 4, half), 0)
+    lane = lax.broadcasted_iota(jnp.int32, (depth * 4, half), 1)
+    target = (row // half) * GROUP + lax.rem(row, GROUP)
+    here = lane == target
+    belongs = lax.rem(row, half) // GROUP
+    cols = jnp.concatenate(
+        [
+            jnp.where(jnp.logical_and(here, belongs == t), 1.0, 0.0).astype(jnp.bfloat16)
+            for t in range(low)
+        ],
+        axis=1,
+    )
 
     by_window = jnp.dot(
         rows_ref[...], a_ref[...], preferred_element_type=jnp.float32
@@ -69,9 +85,8 @@
         ],
         axis=0,
     )
-    turned = jnp.dot(flat, cols_ref[...], preferred_element_type=jnp.float32).astype(jnp.bfloat16)
+    turned = jnp.dot(flat, cols, preferred_element_type=jnp.float32).astype(jnp.bfloat16)
     high = tiles // 2
-    low = groups // high
     for t in range(tiles):
         c, gh = t // high, t % high
         for gl in range(low):
@@ -224,6 +239,8 @@
 
     lax.fori_loop(0, n // 2, others, 0)
 
+    table_copy.wait()
+    pitch = trace.shape[1] // rows
     pk[...] = jnp.zeros_like(pk)
     step = 4
     lanes = pk.shape[1]
@@ -238,7 +255,7 @@
             piece = out[q * rows:(q + 1) * rows]
             for c in range(LAGS // lanes):
                 part = piece[:, c * lanes:(c + 1) * lanes]
-                trace[c, pl.ds(i * step + q, rows, stride=receivers), :] = part
+                trace[c, pl.ds(i * step + q, rows, stride=pitch), :] = part
                 best = jnp.maximum(best, jnp.abs(part))
         pk[...] = best
         return carry
@@ -283,8 +300,9 @@
             row = i * block + q
             factor = inverse[pl.ds(row, 1), :]
             here = pl.ds(pl.multiple_of(row * receivers, receivers), receivers)
+            held_at = pl.ds(pl.multiple_of(row * pitch, 8), receivers)
             for c in range(LAGS // lanes):
-                stage[here, c * lanes:(c + 1) * lanes] = (trace[c, here, :] * factor).astype(
+                stage[here, c * lanes:(c + 1) * lanes] = (trace[c, held_at, :] * factor).astype(
                     jnp.bfloat16
                 )
         o_copy(i).start()
@@ -297,15 +315,11 @@
         o_copy(i).wait()
 
 
-def reorder_tables(receivers, windows, groups):
+def reorder_rows(receivers, windows):
     ch, w = np.meshgrid(np.arange(receivers), np.arange(windows), indexing="ij")
     rows = np.zeros((receivers * windows,) * 2, np.float32)
     rows[(w * receivers + ch).ravel(), (ch * windows + w).ravel()] = 1.0
-    low = 128 // GROUP
-    w, g, f = np.meshgrid(np.arange(windows), np.arange(low), np.arange(GROUP), indexing="ij")
-    cols = np.zeros((windows * 128,) * 2, np.float32)
-    cols[(w * 128 + g * GROUP + f).ravel(), (g * 128 + w * GROUP + f).ravel()] = 1.0
-    return rows.astype(ml_dtypes.bfloat16), cols.astype(ml_dtypes.bfloat16)
+    return rows.astype(ml_dtypes.bfloat16)
 
 
 def fused(n, spectra, blocks, valid, table):
@@ -317,21 +331,22 @@
     per = groups // n
     vmem = pl.BlockSpec(memory_space=pltpu.VMEM)
     smem = pl.BlockSpec(memory_space=pltpu.SMEM)
-    by_row, by_col = reorder_tables(receivers, windows, groups)
+    by_row = reorder_rows(receivers, windows)
     dma = pltpu.SemaphoreType.DMA
     return pl.pallas_call(
         functools.partial(fused_kernel, n),
         out_shape=jax.ShapeDtypeStruct((sources * receivers, LAGS), jnp.bfloat16),
-        in_specs=[vmem, smem, smem, vmem, vmem, vmem],
+        in_specs=[vmem, smem, smem, vmem, pl.BlockSpec(memory_space=pl.ANY)],
         out_specs=pl.BlockSpec(memory_space=pl.ANY),
         scratch_shapes=[
+            pltpu.VMEM(table.shape, table.dtype),
             pltpu.VMEM((groups, receivers, depth), jnp.bfloat16),
             pltpu.VMEM((n, receivers, depth), jnp.bfloat16),
             pltpu.VMEM((n, receivers, depth), jnp.bfloat16),
             pltpu.VMEM((groups, sources, depth), jnp.bfloat16),
             pltpu.VMEM((groups, receivers * 2 * GROUP, depth), jnp.bfloat16),
             pltpu.VMEM((receivers, 2, groups * GROUP, sources), jnp.bfloat16),
-            pltpu.VMEM((LAGS // 128, sources * receivers, 128), jnp.float32),
+            pltpu.VMEM((LAGS // 128, sources * (receivers + 8), 128), jnp.float32),
             pltpu.VMEM((sources * receivers, LAGS), jnp.bfloat16),
             pltpu.VMEM((sources, 128), jnp.float32),
             pltpu.VMEM((n, 8, sources), jnp.float32),
@@ -343,6 +358,7 @@
             dma((n,)),
             dma((n,)),
             dma((chunks,)),
+            dma(()),
         ],
         compiler_params=pltpu.CompilerParams(
             collective_id=0, has_side_effects=True, vmem_limit_bytes=VMEM_LIMIT
@@ -350,7 +366,7 @@
         name="fused",
     )(
         spectra.reshape(receivers * windows, width), blocks, valid,
-        jnp.asarray(by_row), jnp.asarray(by_col), table,
+        jnp.asarray(by_row), table,
     )
 
 

time: 67.6 us -> 59.8 us (0.88)
  Pallas kernels: 62.7 us -> 54.8 us
    pallas_call x1, Pallas kernels: 62.7 us -> 54.8 us  [fused(): pl.pallas_call(functools.partial(fused_kernel, n), out_shape=jax.ShapeDty...]
where the time goes in v3:
time: 59.8 us; the launch traced here: 59.6 us
  Pallas kernels  54.8 us (92%)
  local copies, waits for them, and re-layouts  4.79 us (8%)
    pallas_call x1, Pallas kernels, fused(): pl.pallas_call(functools.partial(fused_kernel, n), out_shape=jax.ShapeDty...  54.8 us
    unnamed x1, local copies, waits for them, and re-layouts  4.79 us

profile of v3, /device:TPU:0, one launch (start us, length us, event | category | flops | bytes accessed | tf_op | source)
XLA Modules:
  0.0 59.6 jit_solution(10503164335098944949)
XLA Ops:
  0.0 54.8 %fused.1 = bf16[4096,512]{1,0:T(8,128)(2,1)} custom-call(bf16[256,1024]{1,0:T(8,128)(2,1)} %bitcast.3, s32[2,2]{1,0:T(2,128)} %blocks_ref.1, s32[8]{0:T(128)} %valid_ref.1, bf16[256,256]{1,0:T(8,128)(2,1)} %constant.5.clone.rows_ref, bf16[1024,512]{1,0:T(8,128)(2,1)} %constant.4.clone.table_hbm), custom_call_target="tpu_custom_call" | custom-call | tf_op jit(solution)/shard_map/fused/pallas_call | solution.py:336
  54.8 4.8 %copy.7 = bf16[2,2,32,32,512]{4,3,2,1,0:T(8,128)(2,1)} copy(bf16[2,2,32,32,512]{4,3,2,1,0:T(8,128)(2,1)} %bitcast.2) | data formatting | bytes 8388608

commit v4 on v3

--- a/solution.py
+++ b/solution.py
@@ -31,7 +31,7 @@
 
 def fused_kernel(
     n, a_ref, blocks_ref, valid_ref, rows_ref, table_hbm, out_ref,
-    table_ref, x, cand0, cand1, held, spread, cross, trace, stage, pk, slots, inverse,
+    table_ref, x, cand0, cand1, held, spread, cross, acc, trace, stage, pk, slots, inverse,
     a_send, a_recv, g_send, g_recv, p_send, p_recv, o_sem, t_sem,
 ):
     me = lax.axis_index("chan")
@@ -159,17 +159,51 @@
     def arrive(cond, h, piece):
         guarded(cond, g_copy(h, piece, c_mate, 0).wait_recv)
 
-    def first(piece):
-        def body(h, carry):
-            g = piece * per + h
+    table_copy.wait()
+    pitch = trace.shape[1] // rows
+    step = acc.shape[1] // rows
+    lanes = pk.shape[1]
+    bundle = groups // 4
+
+    def plane(q, mode):
+        for yy in range(2):
+            for h in range(per):
+                arrive(None, h, index(q, yy, 1 - core))
+
+        def first(j, carry):
+            g = q * bundle + j
             out = lax.dot_general(
                 spread[g], held[g], (((1,), (1,)), ((), ())), preferred_element_type=jnp.float32
             ).astype(jnp.bfloat16)
-            where = pl.ds(pl.multiple_of(g * GROUP, GROUP), GROUP)
+            where = pl.ds(pl.multiple_of(j * GROUP, GROUP), GROUP)
             cross[:, :, where, :] = out.reshape(receivers, 2, GROUP, rows)
             return carry
 
-        lax.fori_loop(0, per, body, 0)
+        lax.fori_loop(0, bundle, first, 0)
+
+        def second(i, carry):
+            parts = [
+                cross[i * step + r].reshape(2 * bundle * GROUP, rows).T for r in range(step)
+            ]
+            out = jnp.dot(
+                jnp.concatenate(parts, axis=0), table_ref[q], preferred_element_type=jnp.float32
+            )
+            if mode == "init":
+                acc[i] = out
+            elif mode == "add":
+                acc[i] += out
+            else:
+                out = out + acc[i]
+                best = pk[...]
+                for r in range(step):
+                    for c in range(LAGS // lanes):
+                        part = out[r * rows:(r + 1) * rows, c * lanes:(c + 1) * lanes]
+                        trace[c, pl.ds(i * step + r, rows, stride=pitch), :] = part
+                        best = jnp.maximum(best, jnp.abs(part))
+                pk[...] = best
+            return carry
+
+        lax.fori_loop(0, receivers // step, second, 0)
 
     for h in range(per):
         for off in range(1, n):
@@ -190,19 +224,11 @@
     def clamp(zz):
         return jnp.clip(zz, 0, 3)
 
-    ready = [(None, me)]
-
     def y_arrived(cond, zz):
         piece = index(zz, 1 - y, core)
         for h in range(per):
             arrive(cond, h, piece)
             send(cond, g_copy(h, piece, c_mate, 3))
-        ready.append((cond, piece))
-
-    def work():
-        for cond, piece in ready:
-            guarded(cond, functools.partial(first, piece))
-        ready.clear()
 
     for d in range(1, 4):
         low_in, low_z = z >= d, clamp(z - d)
@@ -220,47 +246,20 @@
                 send(cond, g_copy(h, piece, c_mate, 3))
         if d == 1:
             y_arrived(None, z)
+            plane(z, "init")
         else:
             y_arrived(z >= d - 1, clamp(z - d + 1))
             y_arrived(z + d - 1 <= 3, clamp(z + d - 1))
-        work()
-        for cond, zz, _, _, _ in ways:
-            ready.append((cond, index(zz, y, core)))
+        if d == 2:
+            pl.when(z >= 1)(functools.partial(plane, clamp(z - 1), "add"))
+            pl.when(z <= 2)(functools.partial(plane, clamp(z + 1), "add"))
+        if d == 3:
+            pl.when(z == 0)(functools.partial(plane, clamp(z + 2), "add"))
+            pl.when(z == 3)(functools.partial(plane, clamp(z - 2), "add"))
     y_arrived(z >= 3, clamp(z - 3))
     y_arrived(z <= 0, clamp(z + 3))
-    work()
-
-    def others(i, carry):
-        piece = index(i // 2, lax.rem(i, 2), 1 - core)
-        for h in range(per):
-            arrive(None, h, piece)
-        first(piece)
-        return carry
-
-    lax.fori_loop(0, n // 2, others, 0)
-
-    table_copy.wait()
-    pitch = trace.shape[1] // rows
     pk[...] = jnp.zeros_like(pk)
-    step = 4
-    lanes = pk.shape[1]
-
-    def second(i, carry):
-        parts = [cross[i * step + q].reshape(2 * groups * GROUP, rows).T for q in range(step)]
-        out = jnp.dot(
-            jnp.concatenate(parts, axis=0), table_ref[...], preferred_element_type=jnp.float32
-        )
-        best = pk[...]
-        for q in range(step):
-            piece = out[q * rows:(q + 1) * rows]
-            for c in range(LAGS // lanes):
-                part = piece[:, c * lanes:(c + 1) * lanes]
-                trace[c, pl.ds(i * step + q, rows, stride=pitch), :] = part
-                best = jnp.maximum(best, jnp.abs(part))
-        pk[...] = best
-        return carry
-
-    lax.fori_loop(0, receivers // step, second, 0)
+    plane(3 - 3 * (z // 2), "last")
 
     own = jnp.max(pk[...].T, axis=0, keepdims=True)
     slots[me] = jnp.broadcast_to(own, slots.shape[1:])
@@ -345,7 +344,8 @@
             pltpu.VMEM((n, receivers, depth), jnp.bfloat16),
             pltpu.VMEM((groups, sources, depth), jnp.bfloat16),
             pltpu.VMEM((groups, receivers * 2 * GROUP, depth), jnp.bfloat16),
-            pltpu.VMEM((receivers, 2, groups * GROUP, sources), jnp.bfloat16),
+            pltpu.VMEM((receivers, 2, groups // 4 * GROUP, sources), jnp.bfloat16),
+            pltpu.VMEM((receivers // 4, 4 * sources, LAGS), jnp.float32),
             pltpu.VMEM((LAGS // 128, sources * (receivers + 8), 128), jnp.float32),
             pltpu.VMEM((sources * receivers, LAGS), jnp.bfloat16),
             pltpu.VMEM((sources, 128), jnp.float32),
@@ -475,7 +475,9 @@
     num_steps = source_blocks.shape[0]
     table = jnp.asarray(build_table(bins, LAGS))
     if n == 16:
-        out = fused(n, spectra, source_blocks, window_valid, table)
+        by_plane = build_table(bins, LAGS).reshape(2, 4, bins // 4, LAGS).transpose(1, 0, 2, 3)
+        by_plane = jnp.asarray(by_plane.reshape(4, bins // 2, LAGS))
+        out = fused(n, spectra, source_blocks, window_valid, by_plane)
     else:
         x = spectra.reshape(receivers, windows, 2, groups, GROUP).transpose(3, 0, 2, 1, 4)
         x = x.reshape(groups, receivers, 2 * windows * GROUP)

time: 59.8 us -> 64.2 us (1.074)
  Pallas kernels: 54.8 us -> 59.2 us
    pallas_call x1, Pallas kernels: 54.8 us -> 59.2 us  [fused(): pl.pallas_call(functools.partial(fused_kernel, n), out_shape=jax.ShapeDty...]
where the time goes in v4:
time: 64.2 us; the launch traced here: 64 us
  Pallas kernels  59.2 us (92%)
  local copies, waits for them, and re-layouts  4.79 us (7%)
    pallas_call x1, Pallas kernels, fused(): pl.pallas_call(functools.partial(fused_kernel, n), out_shape=jax.ShapeDty...  59.2 us
    unnamed x1, local copies, waits for them, and re-layouts  4.79 us

profile of v4, /device:TPU:0, one launch (start us, length us, event | category | flops | bytes accessed | tf_op | source)
XLA Modules:
  0.0 64.0 jit_solution(16274930262144770499)
XLA Ops:
  0.0 59.2 %fused.1 = bf16[4096,512]{1,0:T(8,128)(2,1)} custom-call(bf16[256,1024]{1,0:T(8,128)(2,1)} %bitcast.3, s32[2,2]{1,0:T(2,128)} %blocks_ref.1, s32[8]{0:T(128)} %valid_ref.1, bf16[256,256]{1,0:T(8,128)(2,1)} %constant.5.clone.rows_ref, bf16[4,256,512]{2,1,0:T(8,128)(2,1)} %constant.4.clone.table_hbm), custom_call_target="tpu_custom_call" | custom-call | tf_op jit(solution)/shard_map/fused/pallas_call | solution.py:335
  59.2 4.8 %copy.7 = bf16[2,2,32,32,512]{4,3,2,1,0:T(8,128)(2,1)} copy(bf16[2,2,32,32,512]{4,3,2,1,0:T(8,128)(2,1)} %bitcast.2) | data formatting | bytes 8388608

commit v5 on v3

--- a/solution.py
+++ b/solution.py
@@ -122,7 +122,7 @@
         spread[g] = wide.reshape(receivers * 2 * GROUP, depth)
         return carry
 
-    lax.fori_loop(0, groups, widen, 0)
+    lax.fori_loop(0, groups // 2, widen, 0)
 
     window = lax.rem(lax.broadcasted_iota(jnp.int32, (1, depth), 1), half) // GROUP
     mask = jnp.zeros((1, depth), jnp.float32)
@@ -186,6 +186,8 @@
         send(z > 0, g_copy(h, me, down, 1))
         send(None, g_copy(h, me, y_mate, 2))
         send(None, g_copy(h, me, c_mate, 3))
+        if h == 0:
+            lax.fori_loop(groups // 2, groups, widen, 0)
 
     def clamp(zz):
         return jnp.clip(zz, 0, 3)
@@ -242,7 +244,7 @@
     table_copy.wait()
     pitch = trace.shape[1] // rows
     pk[...] = jnp.zeros_like(pk)
-    step = 4
+    step = 8
     lanes = pk.shape[1]
 
     def second(i, carry):

time: 59.8 us -> 58.9 us (0.985)
  Pallas kernels: 54.8 us -> 54 us
    pallas_call x1, Pallas kernels: 54.8 us -> 54 us  [fused(): pl.pallas_call(functools.partial(fused_kernel, n), out_shape=jax.ShapeDty...]
where the time goes in v5:
time: 58.9 us; the launch traced here: 58.8 us
  Pallas kernels  54 us (92%)
  local copies, waits for them, and re-layouts  4.79 us (8%)
    pallas_call x1, Pallas kernels, fused(): pl.pallas_call(functools.partial(fused_kernel, n), out_shape=jax.ShapeDty...  54 us
    unnamed x1, local copies, waits for them, and re-layouts  4.79 us

profile of v5, /device:TPU:0, one launch (start us, length us, event | category | flops | bytes accessed | tf_op | source)
XLA Modules:
  0.0 58.8 jit_solution(6442934109462951072)
XLA Ops:
  0.0 54.0 %fused.1 = bf16[4096,512]{1,0:T(8,128)(2,1)} custom-call(bf16[256,1024]{1,0:T(8,128)(2,1)} %bitcast.3, s32[2,2]{1,0:T(2,128)} %blocks_ref.1, s32[8]{0:T(128)} %valid_ref.1, bf16[256,256]{1,0:T(8,128)(2,1)} %constant.5.clone.rows_ref, bf16[1024,512]{1,0:T(8,128)(2,1)} %constant.4.clone.table_hbm), custom_call_target="tpu_custom_call" | custom-call | tf_op jit(solution)/shard_map/fused/pallas_call | solution.py:338
  54.0 4.8 %copy.7 = bf16[2,2,32,32,512]{4,3,2,1,0:T(8,128)(2,1)} copy(bf16[2,2,32,32,512]{4,3,2,1,0:T(8,128)(2,1)} %bitcast.2) | data formatting | bytes 8388608
